TPU v7x, 32 devices: a whole 2x2x4 slice. The times are simulated.
32 devices in a mesh: lon: 16 (over z, x, core), lat: 2 (over y).
Axes of the slice: x: 2, y: 2, z: 4, core: 2. Of those that a mesh axis runs over, the one named last changes fastest.
Arguments:
- adjoint_final: float32 [34, 256, 256], P(None, 'lon', 'lat'), may hold values from -6 to 6
- lon_courant: float32 [2, 34, 256, 256], P(None, None, 'lon', 'lat'), may hold values from -0.9 to 0.9
- lon_branch: int32 [2, 34, 256, 256], P(None, None, 'lon', 'lat'), may hold values from 0 to 2
- lat_courant: float32 [2, 34, 256, 256], P(None, None, 'lon', 'lat'), may hold values from -0.9 to 0.9
- lat_branch: int32 [2, 34, 256, 256], P(None, None, 'lon', 'lat'), may hold values from 0 to 2
- mixing: float32 [2, 33, 256, 256], P(None, None, 'lon', 'lat'), may hold values from 0.05 to 5
- region_map: int32 [256, 256], P('lon', 'lat'), may hold values from 0 to 8191
- region_order: int32 [8192], replicated, may hold values from 0 to 8191, each once
- prior_cov: float32 [32, 256, 256], P('lon'), may hold values from -0.4 to 0.4
Outputs:
- adjoint_start: float32 [34, 256, 256], P(None, 'lon', 'lat')
- flux_gradient: float32 [2, 8192], P(None, ('lon', 'lat'))
Inputs may be any that keep to these rules, and one draw needn't show every extreme that they name: `region_order`: each position appears once.
All inputs are finite; a program needn't handle non-finite values.
Results may differ from a plain program's by a relative error of at most 0.0003.
Values sent between devices are 32-bit elements; how exact they have to be, the bound alone decides.
A program may use at most 128 MiB of HBM per device.

v0:
```python
import math

import jax
import jax.numpy as jnp
from jax import lax
from jax.sharding import PartitionSpec as P


def extended(cells, sides, width, closed):
    for axis, dim in sides:
        count = lax.axis_size(axis)
        ends = count if closed else count - 1
        head = lax.slice_in_dim(cells, 0, width, axis=dim)
        tail = lax.slice_in_dim(cells, cells.shape[dim] - width, cells.shape[dim], axis=dim)
        cells = jnp.concatenate(
            [
                lax.ppermute(tail, axis, [(i, (i + 1) % count) for i in range(ends)]),
                cells,
                lax.ppermute(head, axis, [((i + 1) % count, i) for i in range(ends)]),
            ],
            axis=dim,
        )
    return cells


def face_weights(courant, branch):
    half_step = 0.5 * (1.0 - jnp.abs(courant))
    lean_part = courant * half_step
    branch_one = jnp.where(branch == 1, 1.0, 0.0)
    branch_two = jnp.where(branch == 2, 1.0, 0.0)
    upwind_left = jnp.where(courant > 0.0, 1.0, 0.0)
    upwind_right = 1.0 - upwind_left
    donor = courant - branch_one * lean_part + branch_two * lean_part
    weight_far = -(upwind_left * branch_two * lean_part)
    weight_left = upwind_left * donor + upwind_right * branch_one * lean_part
    weight_right = upwind_left * branch_one * lean_part + upwind_right * donor
    weight_next = -(upwind_right * branch_two * lean_part)
    return [weight_far, weight_left, weight_right, weight_next]


def window(array, start, count, axis):
    return lax.slice_in_dim(array, start, start + count, axis=axis)


def transpose_flux(adjoint, padded, weights, axis):
    count = adjoint.shape[axis]
    jumps = window(padded, 1, count + 3, axis) - window(padded, 0, count + 3, axis)
    terms = [window(weight, 1, count + 3, axis) * jumps for weight in weights]
    result = adjoint + window(terms[0], 3, count, axis)
    result = result + window(terms[1], 2, count, axis)
    result = result + window(terms[2], 1, count, axis)
    return result + window(terms[3], 0, count, axis)


def vertical_solve(rhs, mixing):
    level_count = rhs.shape[0]
    ratios = []
    carried = []
    for level in range(level_count):
        if level == 0:
            denom = 1.0 + mixing[0]
            value = rhs[0] / denom
        else:
            lower = mixing[level - 1]
            diagonal = 1.0 + lower + mixing[level] if level < level_count - 1 else 1.0 + lower
            denom = diagonal + lower * ratios[-1]
            value = (rhs[level] + lower * carried[-1]) / denom
        ratios.append(-mixing[level] / denom if level < level_count - 1 else None)
        carried.append(value)
    result = [carried[-1]]
    for level in range(level_count - 2, -1, -1):
        result.insert(0, carried[level] - ratios[level] * result[0])
    return jnp.stack(result)


def weight_table(courant, branch):
    return jnp.stack(
        [jnp.stack(face_weights(courant[step], branch[step])) for step in range(courant.shape[0])]
    )


def per_device(
    adjoint_final,
    lon_courant,
    lon_branch,
    lat_courant,
    lat_branch,
    mixing,
    region_map,
    region_order,
    prior_cov,
):
    step_count, level_count, lon_cells, lat_cells = lon_courant.shape
    lat_total = lat_cells * lax.axis_size("lat")
    lat_index = lax.axis_index("lat") * lat_cells + jnp.arange(lat_cells, dtype=jnp.int32)
    coslat = jnp.cos((lat_index.astype(jnp.float32) + 0.5) * (math.pi / lat_total) - 0.5 * math.pi)
    lat_inner = jnp.where(lat_index == 0, 0.0, lat_courant)
    surface = [None] * step_count
    adjoint = adjoint_final
    lon_padded = extended(weight_table(lon_courant, lon_branch), (("lon", 3),), 2, True)
    lat_padded = extended(weight_table(lat_inner, lat_branch), (("lat", 4),), 2, False)
    for step in range(step_count - 1, -1, -1):
        adjoint = vertical_solve(adjoint, mixing[step])
        padded = extended(adjoint, (("lat", 2),), 2, False)
        adjoint = transpose_flux(
            adjoint, padded, [lat_padded[step, member] for member in range(4)], 2
        )
        padded = extended(adjoint, (("lon", 1),), 2, True)
        adjoint = transpose_flux(
            adjoint, padded, [lon_padded[step, member] for member in range(4)], 1
        )
        surface[step] = adjoint[0] * coslat[None, :]
    cell_count = lon_cells * lat_cells
    field = jnp.stack(surface).reshape(step_count, cell_count)
    slots = jnp.take(region_order, region_map.reshape(cell_count), axis=0)
    regions = region_order.shape[0]
    row_count = regions // 128
    row_hit = jnp.where(
        (slots // 128)[:, None] == jnp.arange(row_count, dtype=jnp.int32)[None, :], 1.0, 0.0
    )
    col_hit = jnp.where(
        (slots % 128)[:, None] == jnp.arange(128, dtype=jnp.int32)[None, :], 1.0, 0.0
    )
    spread = field[:, :, None] * row_hit[None, :, :]
    partial_value = jnp.einsum(
        "scr,ck->srk", spread, col_hit, precision=lax.Precision.HIGHEST
    ).reshape(step_count, regions)
    share = lax.psum_scatter(partial_value, ("lon", "lat"), scatter_dimension=1, tiled=True)
    group = lax.all_gather(share, "lat", axis=1, tiled=True)
    block_count = prior_cov.shape[0]
    block_size = prior_cov.shape[1]
    blocks = group.reshape(step_count, block_count, block_size)
    mapped = jnp.einsum("sbj,bji->sbi", blocks, prior_cov, precision=lax.Precision.HIGHEST)
    mapped = mapped.reshape(step_count, block_count * block_size)
    own_width = block_count * block_size // lax.axis_size("lat")
    result = lax.dynamic_slice_in_dim(mapped, lax.axis_index("lat") * own_width, own_width, 1)
    return (adjoint, result)


def solution(mesh):
    placed = (
        P(None, "lon", "lat"),
        P(None, None, "lon", "lat"),
        P(None, None, "lon", "lat"),
        P(None, None, "lon", "lat"),
        P(None, None, "lon", "lat"),
        P(None, None, "lon", "lat"),
        P("lon", "lat"),
        P(),
        P("lon", None, None),
    )
    return jax.shard_map(
        per_device,
        mesh=mesh,
        in_specs=placed,
        out_specs=(P(None, "lon", "lat"), P(None, ("lon", "lat"))),
        check_vma=False,
    )
```

profile of v0, /device:TPU:0, one launch (start us, length us, event | category | flops | bytes accessed | tf_op | source)
XLA Modules:
  0.0 259.7 jit_solution(2476000642928047329)
XLA Ops:
  7.2 1.5 fusion.181
  8.7 1.1 constant_dynamic-update-slice_fusion.33
  10.2 0.7 constant_dynamic-update-slice_fusion.1
  11.0 0.7 constant_dynamic-update-slice_fusion
  11.7 0.7 copy-done.5
  12.4 0.9 fusion.431
  13.3 1.3 collective-permute-start.3
  14.6 6.3 %collective-permute-start.2 = (f32[34,16,2]{2,1,0:T(8,128)}, f32[34,16,2]{2,1,0:T(8,128)}, u32[]{:S(2)}, u32[]{:S(2)}) collective-permute-start(f32[34,16,2]{2,1,0:T(8,128)} %get-tuple-element.228), channel_id=1, source_target_pairs={{0,1},{2,3},{4,5},{6,7},{8,9},{10,11},{12,13},{14,15},{16,17},{18,... | collective-permute-start | bytes 13064 | tf_op jit(solution)/shard_map/ppermute | solution.py:17
  21.3 0.5 fusion.23
  21.7 0.4 fusion.17
  22.4 2.2 slice_maximum_fusion
  24.5 2.7 %copy.120 = f32[2,4,34,16,2]{2,3,4,1,0:T(8,128)S(1)} copy(f32[2,4,34,16,2]{4,3,2,1,0:T(8,128)} %get-tuple-element.201) | data formatting | bytes 69632 | tf_op jit(solution)/shard_map/slice | solution.py:13
  27.2 1.3 collective-permute-start.1
  28.5 1.7 copy.119
  30.3 6.0 %collective-permute-start = (f32[2,4,34,16,2]{2,3,4,1,0:T(8,128)}, f32[2,4,34,16,2]{2,3,4,1,0:T(8,128)}, u32[]{:S(2)}, u32[]{:S(2)}) collective-permute-start(f32[2,4,34,16,2]{2,3,4,1,0:T(8,128)} %copy.119), channel_id=1, source_target_pairs={{0,1},{2,3},{4,5},{6,7},{8,9},{10,11},{12,13},{14,15},{16,17},{18,... | collective-permute-start | bytes 104456 | tf_op jit(solution)/shard_map/ppermute | solution.py:17
  36.2 1.4 fusion.49
  37.6 0.5 fusion.35
  38.1 0.4 fusion.15
  38.7 1.0 pad_maximum_fusion.8
  39.7 4.0 %collective-permute-start.5 = (f32[2,4,34,2,128]{4,3,2,1,0:T(2,128)}, f32[2,4,34,2,128]{4,3,2,1,0:T(2,128)}, u32[]{:S(2)}, u32[]{:S(2)}) collective-permute-start(f32[2,4,34,2,128]{4,3,2,1,0:T(2,128)} %get-tuple-element.199), channel_id=1, source_target_pairs={{2,0},{4,2},{6,4},{8,6},{10,8},{12,10},{14,12},{16,14},{18,16},{20... | collective-permute-start | bytes 835592 | tf_op jit(solution)/shard_map/ppermute | solution.py:19
  44.0 1.3 pad_maximum_fusion.3
  45.5 3.3 %copy.122 = f32[2,4,34,16,2]{4,3,2,1,0:T(8,128)} copy(f32[2,4,34,16,2]{2,3,4,1,0:T(8,128)} %collective-permute-done.1) | data formatting | bytes 69632 | tf_op jit(solution)/shard_map/ppermute | solution.py:19
  48.9 3.3 %copy.121 = f32[2,4,34,16,2]{4,3,2,1,0:T(8,128)} copy(f32[2,4,34,16,2]{2,3,4,1,0:T(8,128)} %collective-permute-done) | data formatting | bytes 69632 | tf_op jit(solution)/shard_map/ppermute | solution.py:17
  52.2 4.8 %pad_maximum_fusion = f32[2,4,34,16,132]{4,3,2,1,0:T(8,128)S(1)} fusion(f32[2,4,34,16,2]{4,3,2,1,0:T(8,128)} %copy.122, f32[1,4,34,16,128]{4,3,2,1,0:T(8,128)} %copy-done.3, f32[1,4,34,16,128]{4,3,2,1,0:T(8,128)} %copy-done.2, f32[2,4,34,16,2]{4,3,2,1,0:T(8,128)} %copy.121), kind=kLoop, calls=%fused_computation.1 | loop fusion | flops 1723392 | bytes 4595712 | tf_op jit(solution)/shard_map/concatenate | solution.py:15
  57.0 1.7 slice_bitcast_fusion.3
  59.5 0.5 copy-done.7
  60.1 0.5 fusion.66
  60.6 0.7 copy-done.8
  61.3 4.5 %collective-permute-start.7 = (f32[34,2,128]{2,1,0:T(2,128)S(1)}, f32[34,2,128]{2,1,0:T(2,128)S(1)}, u32[]{:S(2)}, u32[]{:S(2)}) collective-permute-start(f32[34,2,128]{2,1,0:T(2,128)S(1)} %get-tuple-element.227), channel_id=1, source_target_pairs={{2,0},{4,2},{6,4},{8,6},{10,8},{12,10},{14,12},{16,14},{18,16},{20... | collective-permute-start | bytes 104456 | tf_op jit(solution)/shard_map/ppermute | solution.py:19
  65.8 11.8 %gather_fusion = s32[2048]{0:T(1024)S(1)} fusion(s32[8192]{0:T(1024)S(1)} %copy-done.1, s32[2048]{0:T(1024)S(1)} %broadcast_clamp_fusion), kind=kCustom, calls=%fused_computation | custom fusion | bytes 24576 | tf_op jit(solution)/shard_map/jit(_take)/gather | solution.py:115
  77.8 1.5 pad_maximum_fusion.1
  80.0 0.8 copy-done.16
  81.8 1.4 collective-permute-start.9
  83.2 4.6 %collective-permute-start.8 = (f32[34,16,2]{2,1,0:T(8,128)S(1)}, f32[34,16,2]{2,1,0:T(8,128)S(1)}, u32[]{:S(2)}, u32[]{:S(2)}) collective-permute-start(f32[34,16,2]{2,1,0:T(8,128)S(1)} %get-tuple-element.224), channel_id=1, source_target_pairs={{0,1},{2,3},{4,5},{6,7},{8,9},{10,11},{12,13},{14,15},{16,17},{18,... | collective-permute-start | bytes 13064 | tf_op jit(solution)/shard_map/ppermute | solution.py:17
  88.3 0.6 copy-done.11
  89.4 1.0 collective-permute-done.9
  90.4 1.5 collective-permute-done.8
  92.4 0.5 fusion.58
  92.9 3.4 %collective-permute-start.11 = (f32[34,2,128]{2,1,0:T(2,128)S(1)}, f32[34,2,128]{2,1,0:T(2,128)S(1)}, u32[]{:S(2)}, u32[]{:S(2)}) collective-permute-start(f32[34,2,128]{2,1,0:T(2,128)S(1)} %get-tuple-element.223), channel_id=1, source_target_pairs={{2,0},{4,2},{6,4},{8,6},{10,8},{12,10},{14,12},{16,14},{18,16},{20... | collective-permute-start | bytes 104456 | tf_op jit(solution)/shard_map/ppermute | solution.py:19
  96.5 1.4 collective-permute-done.11
  97.9 4.4 %collective-permute-done.10 = f32[34,2,128]{2,1,0:T(2,128)S(1)} collective-permute-done((f32[34,2,128]{2,1,0:T(2,128)S(1)}, f32[34,2,128]{2,1,0:T(2,128)S(1)}, u32[]{:S(2)}, u32[]{:S(2)}) %collective-permute-start.10) | collective-permute-done | bytes 34848 | tf_op jit(solution)/shard_map/ppermute | solution.py:17
  102.7 1.4 fusion
  104.1 2.7 %copy.125 = f32[2,64,128]{0,2,1:T(8,128)} copy(f32[2,64,128]{2,1,0:T(8,128)S(1)} %fusion) | data formatting | bytes 131072
  106.8 139.8 %reduce-scatter.4.cloned.1.call-done = f32[256,2]{1,0:T(8,128)} async-done(((f32[8192,2]{1,0:T(8,128)}), f32[256,2]{1,0:T(8,128)}) %reduce-scatter.4.cloned.1.call-update) | async-done | bytes 2064
  246.5 1.0 copy.124
  247.5 4.3 %all_gather.3 = f32[2,512]{1,0:T(2,128)S(1)} all-gather(f32[2,256]{1,0:T(2,128)S(1)} %copy.124), channel_id=1, replica_groups=mesh['lon'=16,'lat'=2] {'lat'}, dimensions={1}, use_global_device_ids=true | all-gather | bytes 6144 | tf_op jit(solution)/shard_map/all_gather | solution.py:129
  251.9 0.4 fusion.432
  252.2 0.6 constant_dynamic-slice_fusion
  (156 shorter events, 5.7 us)
Async XLA Ops:
  7.2 244.7 %copy-start = (f32[2,256,256]{2,1,0:T(8,128)S(1)}, f32[2,256,256]{2,1,0:T(8,128)}, u32[]{:S(2)}) copy-start(f32[2,256,256]{2,1,0:T(8,128)} %param.17) | copy-start | bytes 1572868
  7.2 239.4 %reduce-scatter.4.cloned.1.call-start = ((), (), s32[]{:S(2)}) async-start(), calls=%async_computation.1 | async-start | bytes 4325376
  9.8 11.0 %copy-start.17 = (f32[2,34,16,128]{3,2,1,0:T(8,128)S(1)}, f32[2,34,16,128]{3,2,1,0:T(8,128)}, u32[]{:S(2)}) copy-start(f32[2,34,16,128]{3,2,1,0:T(8,128)} %param.12) | copy-start | bytes 1671172
  11.7 0.7 copy-start.5
  12.4 8.5 %copy-start.14 = (s32[2,34,16,128]{3,2,1,0:T(8,128)S(1)}, s32[2,34,16,128]{3,2,1,0:T(8,128)}, u32[]{:S(2)}) copy-start(s32[2,34,16,128]{3,2,1,0:T(8,128)} %param.13) | copy-start | bytes 1671172
  13.3 30.4 %collective-permute-start.3 = (f32[34,16,2]{2,1,0:T(8,128)}, f32[34,16,2]{2,1,0:T(8,128)}, u32[]{:S(2)}, u32[]{:S(2)}) collective-permute-start(f32[34,16,2]{2,1,0:T(8,128)} %get-tuple-element.229), channel_id=1, source_target_pairs={{1,0},{3,2},{5,4},{7,6},{9,8},{11,10},{13,12},{15,14},{17,16},{19,... | collective-permute-start | bytes 13064 | tf_op jit(solution)/shard_map/ppermute | solution.py:19
  14.6 29.4 %collective-permute-start.2 = (f32[34,16,2]{2,1,0:T(8,128)}, f32[34,16,2]{2,1,0:T(8,128)}, u32[]{:S(2)}, u32[]{:S(2)}) collective-permute-start(f32[34,16,2]{2,1,0:T(8,128)} %get-tuple-element.228), channel_id=1, source_target_pairs={{0,1},{2,3},{4,5},{6,7},{8,9},{10,11},{12,13},{14,15},{16,17},{18,... | collective-permute-start | bytes 13064 | tf_op jit(solution)/shard_map/ppermute | solution.py:17
  22.3 2.2 copy-start.2
  22.4 2.2 copy-start.3
  27.2 18.3 %collective-permute-start.1 = (f32[2,4,34,16,2]{2,3,4,1,0:T(8,128)S(1)}, f32[2,4,34,16,2]{2,3,4,1,0:T(8,128)}, u32[]{:S(2)}, u32[]{:S(2)}) collective-permute-start(f32[2,4,34,16,2]{2,3,4,1,0:T(8,128)S(1)} %copy.120), channel_id=1, source_target_pairs={{1,0},{3,2},{5,4},{7,6},{9,8},{11,10},{13,12},{15,14},{17,16},{19,... | collective-permute-start | bytes 104456 | tf_op jit(solution)/shard_map/ppermute | solution.py:19
  28.5 7.7 %copy-start.4 = (f32[2,34,16,128]{3,2,1,0:T(8,128)S(1)}, f32[2,34,16,128]{3,2,1,0:T(8,128)}, u32[]{:S(2)}) copy-start(f32[2,34,16,128]{3,2,1,0:T(8,128)} %param.10) | copy-start | bytes 1671172
  30.3 7.3 %copy-start.15 = (s32[2,34,16,128]{3,2,1,0:T(8,128)S(1)}, s32[2,34,16,128]{3,2,1,0:T(8,128)}, u32[]{:S(2)}) copy-start(s32[2,34,16,128]{3,2,1,0:T(8,128)} %param.11) | copy-start | bytes 1671172
  30.3 18.6 %collective-permute-start = (f32[2,4,34,16,2]{2,3,4,1,0:T(8,128)}, f32[2,4,34,16,2]{2,3,4,1,0:T(8,128)}, u32[]{:S(2)}, u32[]{:S(2)}) collective-permute-start(f32[2,4,34,16,2]{2,3,4,1,0:T(8,128)} %copy.119), channel_id=1, source_target_pairs={{0,1},{2,3},{4,5},{6,7},{8,9},{10,11},{12,13},{14,15},{16,17},{18,... | collective-permute-start | bytes 104456 | tf_op jit(solution)/shard_map/ppermute | solution.py:17
  38.7 5.0 %copy-start.19 = (s32[16,128]{1,0:T(8,128)S(1)}, s32[16,128]{1,0:T(8,128)}, u32[]{:S(2)}) copy-start(s32[16,128]{1,0:T(8,128)} %param.15) | copy-start | bytes 24580
  38.7 5.3 %copy-start.6 = (f32[34,16,128]{2,1,0:T(8,128)S(1)}, f32[34,16,128]{2,1,0:T(8,128)}, u32[]{:S(2)}) copy-start(f32[34,16,128]{2,1,0:T(8,128)} %copy-done.5) | copy-start | bytes 835588
  39.7 38.1 %collective-permute-start.5 = (f32[2,4,34,2,128]{4,3,2,1,0:T(2,128)}, f32[2,4,34,2,128]{4,3,2,1,0:T(2,128)}, u32[]{:S(2)}, u32[]{:S(2)}) collective-permute-start(f32[2,4,34,2,128]{4,3,2,1,0:T(2,128)} %get-tuple-element.199), channel_id=1, source_target_pairs={{2,0},{4,2},{6,4},{8,6},{10,8},{12,10},{14,12},{16,14},{18,16},{20... | collective-permute-start | bytes 835592 | tf_op jit(solution)/shard_map/ppermute | solution.py:19
  43.7 34.1 %collective-permute-start.4 = (f32[2,4,34,2,128]{4,3,2,1,0:T(2,128)}, f32[2,4,34,2,128]{4,3,2,1,0:T(2,128)}, u32[]{:S(2)}, u32[]{:S(2)}) collective-permute-start(f32[2,4,34,2,128]{4,3,2,1,0:T(2,128)} %get-tuple-element.198), channel_id=1, source_target_pairs={{0,2},{2,4},{4,6},{6,8},{8,10},{10,12},{12,14},{14,16},{16,18},{18... | collective-permute-start | bytes 835592 | tf_op jit(solution)/shard_map/ppermute | solution.py:17
  59.1 1.0 copy-start.7
  60.1 5.8 %copy-start.1 = (s32[8192]{0:T(1024)S(1)}, s32[8192]{0:T(1024)}, u32[]{:S(2)}) copy-start(s32[8192]{0:T(1024)} %param.16) | copy-start | bytes 98308
  60.6 0.7 copy-start.8
  61.3 16.3 %collective-permute-start.7 = (f32[34,2,128]{2,1,0:T(2,128)S(1)}, f32[34,2,128]{2,1,0:T(2,128)S(1)}, u32[]{:S(2)}, u32[]{:S(2)}) collective-permute-start(f32[34,2,128]{2,1,0:T(2,128)S(1)} %get-tuple-element.227), channel_id=1, source_target_pairs={{2,0},{4,2},{6,4},{8,6},{10,8},{12,10},{14,12},{16,14},{18,16},{20... | collective-permute-start | bytes 104456 | tf_op jit(solution)/shard_map/ppermute | solution.py:19
  65.8 11.9 %collective-permute-start.6 = (f32[34,2,128]{2,1,0:T(2,128)S(1)}, f32[34,2,128]{2,1,0:T(2,128)S(1)}, u32[]{:S(2)}, u32[]{:S(2)}) collective-permute-start(f32[34,2,128]{2,1,0:T(2,128)S(1)} %get-tuple-element.226), channel_id=1, source_target_pairs={{0,2},{2,4},{4,6},{6,8},{8,10},{10,12},{12,14},{14,16},{16,18},{18... | collective-permute-start | bytes 104456 | tf_op jit(solution)/shard_map/ppermute | solution.py:17
  65.8 11.8 %copy-start.9 = (f32[34,16,128]{2,1,0:T(8,128)S(1)}, f32[34,16,128]{2,1,0:T(8,128)}, u32[]{:S(2)}) copy-start(f32[34,16,128]{2,1,0:T(8,128)} %copy-done.8) | copy-start | bytes 835588
  79.7 1.1 copy-start.16
  81.2 6.6 %copy-start.13 = (f32[34,16,132]{2,1,0:T(8,128)S(1)}, f32[34,16,132]{2,1,0:T(8,128)}, u32[]{:S(2)}) copy-start(f32[34,16,132]{2,1,0:T(8,128)} %get-tuple-element.183) | copy-start | bytes 861700
  81.7 6.4 %copy-start.12 = (f32[34,16,132]{2,1,0:T(8,128)S(1)}, f32[34,16,132]{2,1,0:T(8,128)}, u32[]{:S(2)}) copy-start(f32[34,16,132]{2,1,0:T(8,128)} %get-tuple-element.184) | copy-start | bytes 861700
  81.8 8.6 %collective-permute-start.9 = (f32[34,16,2]{2,1,0:T(8,128)S(1)}, f32[34,16,2]{2,1,0:T(8,128)S(1)}, u32[]{:S(2)}, u32[]{:S(2)}) collective-permute-start(f32[34,16,2]{2,1,0:T(8,128)S(1)} %get-tuple-element.225), channel_id=1, source_target_pairs={{1,0},{3,2},{5,4},{7,6},{9,8},{11,10},{13,12},{15,14},{17,16},{19,... | collective-permute-start | bytes 13064 | tf_op jit(solution)/shard_map/ppermute | solution.py:19
  83.2 8.6 %collective-permute-start.8 = (f32[34,16,2]{2,1,0:T(8,128)S(1)}, f32[34,16,2]{2,1,0:T(8,128)S(1)}, u32[]{:S(2)}, u32[]{:S(2)}) collective-permute-start(f32[34,16,2]{2,1,0:T(8,128)S(1)} %get-tuple-element.224), channel_id=1, source_target_pairs={{0,1},{2,3},{4,5},{6,7},{8,9},{10,11},{12,13},{14,15},{16,17},{18,... | collective-permute-start | bytes 13064 | tf_op jit(solution)/shard_map/ppermute | solution.py:17
  87.9 1.1 copy-start.11
  88.1 1.1 copy-start.10
  92.9 5.0 %collective-permute-start.11 = (f32[34,2,128]{2,1,0:T(2,128)S(1)}, f32[34,2,128]{2,1,0:T(2,128)S(1)}, u32[]{:S(2)}, u32[]{:S(2)}) collective-permute-start(f32[34,2,128]{2,1,0:T(2,128)S(1)} %get-tuple-element.223), channel_id=1, source_target_pairs={{2,0},{4,2},{6,4},{8,6},{10,8},{12,10},{14,12},{16,14},{18,16},{20... | collective-permute-start | bytes 104456 | tf_op jit(solution)/shard_map/ppermute | solution.py:19
  96.3 6.1 %collective-permute-start.10 = (f32[34,2,128]{2,1,0:T(2,128)S(1)}, f32[34,2,128]{2,1,0:T(2,128)S(1)}, u32[]{:S(2)}, u32[]{:S(2)}) collective-permute-start(f32[34,2,128]{2,1,0:T(2,128)S(1)} %get-tuple-element.222), channel_id=1, source_target_pairs={{0,2},{2,4},{4,6},{6,8},{8,10},{10,12},{12,14},{14,16},{16,18},{18... | collective-permute-start | bytes 104456 | tf_op jit(solution)/shard_map/ppermute | solution.py:17
  102.6 4.1 %copy-start.18 = (f32[34,16,128]{2,1,0:T(8,128)}, f32[34,16,128]{2,1,0:T(8,128)S(1)}, u32[]{:S(2)}) copy-start(f32[34,16,128]{2,1,0:T(8,128)S(1)} %fusion.54) | copy-start | bytes 835588
Sparse Core Ops, SparseCore 0:
  106.9 139.5 reduce-scatter.3
where the time goes:
time: 260 us
  waiting for transfers between devices  148 us (57%)
  local copies, waits for them, and re-layouts  35.6 us (14%)
  starting transfers between devices  32.9 us (13%)
  other arithmetic  21.8 us (8%)
  between operations  15.1 us (6%)
  blocking collectives  4.34 us (2%)
    unnamed x2, waiting for transfers between devices  140 us
    ppermute x6, starting transfers between devices, extended(): lax.ppermute(tail, axis, [(i, (i + 1) % count) for i in range(ends)])  17.1 us
    ppermute x6, starting transfers between devices, extended(): lax.ppermute(head, axis, [((i + 1) % count, i) for i in range(ends)])  15.8 us
    gather x1, local copies, waits for them, and re-layouts, per_device(): slots = jnp.take(region_order, region_map.reshape(cell_count), axis=0)  11.8 us
    concatenate x6, other arithmetic, extended(): jnp.concatenate([lax.ppermute(tail, axis, [(i, (i + 1) % count) for i in...  8.05 us
    unnamed x75, local copies, waits for them, and re-layouts  7.29 us
    ppermute x6, waiting for transfers between devices, extended(): lax.ppermute(tail, axis, [(i, (i + 1) % count) for i in range(ends)])  5.93 us
  transfers between devices with their start and end apart: 13, of which 5 were waited for; matrix products, arithmetic and copies ran while one was open for 16% of the time, Pallas kernels for 0%

commit v1 on v0

v1 whole, which is shorter than its diff:
```python
import functools
import math

import jax
import jax.numpy as jnp
import numpy as np
from jax import lax
from jax.experimental import pallas as pl
from jax.experimental.pallas import tpu as pltpu
from jax.sharding import PartitionSpec as P

MESH = pl.DeviceIdType.MESH
OWN = 8


def face_weights(courant, branch):
    lean_part = courant * (0.5 * (1.0 - jnp.abs(courant)))
    one_part = jnp.where(branch == 1, lean_part, 0.0)
    two_part = jnp.where(branch == 2, lean_part, 0.0)
    donor = courant - one_part + two_part
    left = courant > 0.0
    return (
        jnp.where(left, -two_part, 0.0),
        jnp.where(left, donor, one_part),
        jnp.where(left, one_part, donor),
        jnp.where(left, 0.0, -two_part),
    )


def kernel(
    nlon,
    nlat,
    width,
    adj_h,
    lonc_h,
    lonb_h,
    latc_h,
    latb_h,
    mix_h,
    cov_h,
    rmap_ref,
    order_ref,
    cos_ref,
    out_ref,
    flux_ref,
    x_ref,
    mixv,
    latc,
    latb,
    lonc,
    lonb,
    covv,
    inv_ref,
    kin_ref,
    nr_ref,
    y_ref,
    ext,
    lw,
    pack_w,
    land_w,
    pack_a,
    land_a,
    hi_ref,
    lo_ref,
    cht,
    amat,
    pscr,
    send_ref,
    land,
    local_sem,
    send_sem,
    recv_sem,
    all_sem,
):
    steps, levels, rows, lanes = latc.shape
    count = nlon * nlat
    my_lon, my_lat = lax.axis_index("lon"), lax.axis_index("lat")
    me = my_lon * nlat + my_lat
    blk = covv.shape[0]

    def place(device):
        return (device // nlat, lax.rem(device, nlat))

    barrier = pltpu.get_barrier_semaphore()

    def greet(k, carry):
        pl.semaphore_signal(
            barrier, inc=1, device_id=place(lax.rem(me + k, count)), device_id_type=MESH
        )
        return carry

    lax.fori_loop(1, count, greet, 0)

    def fetch(src, dst, slot):
        copy = pltpu.make_async_copy(src, dst, local_sem.at[slot])
        copy.start()
        return copy

    own = pl.ds(OWN, rows)
    get_mix = [None, None]
    get_mix[1] = fetch(mix_h.at[1], mixv.at[1], 0)
    get_adj = fetch(adj_h, x_ref, 1)
    get_latc = fetch(latc_h, latc, 2)
    get_latb = fetch(latb_h, latb, 3)
    get_lonc = fetch(lonc_h, lonc.at[:, :, own, :], 4)
    get_lonb = fetch(lonb_h, lonb.at[:, :, own, :], 5)
    get_mix[0] = fetch(mix_h.at[0], mixv.at[0], 6)
    get_cov = fetch(cov_h.at[(my_lat * width) // blk], covv, 7)

    lane = lax.broadcasted_iota(jnp.int32, (rows, lanes), 1)
    pair = lane // 2
    even = lax.rem(lane, 2) == 0
    zero = jnp.zeros((rows, lanes), jnp.float32)

    def roll(value, shift):
        return pltpu.roll(value, shift, 1)

    def remote(src, dst, slot, device):
        copy = pltpu.make_async_remote_copy(
            src_ref=src,
            dst_ref=dst,
            send_sem=send_sem.at[slot],
            recv_sem=recv_sem.at[slot],
            device_id=device,
            device_id_type=MESH,
        )
        copy.start()
        return copy

    north = (my_lon, lax.rem(my_lat + 1, nlat))
    south = (my_lon, lax.rem(my_lat + nlat - 1, nlat))
    east = (lax.rem(my_lon + 1, nlon), my_lat)
    west = (lax.rem(my_lon + nlon - 1, nlon), my_lat)

    def coefficients(s):
        k = mixv[s, 0]
        inv = 1.0 / (1.0 + k)
        inv_ref[s, 0] = inv
        kin_ref[s, 0] = zero
        nr_ref[s, 0] = k * inv

        def body(level, ahead):
            lower, k = mixv[s, level - 1], mixv[s, level]
            inv = 1.0 / ((1.0 + k) + lower * (1.0 - ahead))
            inv_ref[s, level] = inv
            kin_ref[s, level] = lower * inv
            ahead = k * inv
            nr_ref[s, level] = ahead
            return ahead

        ahead = lax.fori_loop(1, levels - 1, body, k * inv, unroll=True)
        lower = mixv[s, levels - 2]
        inv = 1.0 / (1.0 + lower * (1.0 - ahead))
        inv_ref[s, levels - 1] = inv
        kin_ref[s, levels - 1] = lower * inv
        nr_ref[s, levels - 1] = zero

    def tail_head(value, level, tail, head):
        turned = roll(value, 2 * level + 2)
        return jnp.where(pair == level, turned, tail), jnp.where(pair == level + 1, turned, head)

    def solve(s):
        def up(level, carried):
            carried = x_ref[level] * inv_ref[s, level] + kin_ref[s, level] * carried
            y_ref[level] = carried
            return carried

        lax.fori_loop(0, levels, up, zero, unroll=True)

        def down(i, carry):
            value, tail, head = carry
            level = levels - 1 - i
            value = y_ref[level] + nr_ref[s, level] * value
            y_ref[level] = value
            return (value,) + tail_head(value, level, tail, head)

        _, tail, head = lax.fori_loop(0, levels, down, (zero, zero, zero), unroll=True)
        pack_a[s, 0] = tail
        pack_a[s, 1] = roll(head, lanes - 2)

    def pack_weights(s):
        def body(level, carry):
            ct, ch, bt, bh = carry
            ct, ch = tail_head(latc[s, level], level, ct, ch)
            bt, bh = tail_head(latb[s, level].astype(jnp.float32), level, bt, bh)
            return ct, ch, bt, bh

        ct, ch, bt, bh = lax.fori_loop(0, levels, body, (zero,) * 4, unroll=True)
        pack_w[0, s, 0] = ct
        pack_w[0, s, 1] = bt
        pack_w[1, s, 0] = roll(ch, lanes - 2)
        pack_w[1, s, 1] = roll(bh, lanes - 2)

    def lat_inner(s):
        def body(level, carry):
            a = y_ref[level]
            m2, m1, m0, p1 = face_weights(latc[s, level], latb[s, level])
            jump = jnp.where(lane >= 1, a - roll(a, 1), 0.0)
            out = a + m0 * jump + roll(m1 * jump, lanes - 1)
            out = out + roll(jnp.where(lane >= 2, m2 * jump, 0.0), lanes - 2)
            out = out + roll(jnp.where(lane <= lanes - 2, p1 * jump, 0.0), 1)
            ext[s, level, OWN : OWN + rows] = out
            return carry

        lax.fori_loop(0, levels, body, 0, unroll=True)

    def lat_edges(s):
        tail, head = pack_a[s, 0], pack_a[s, 1]
        before, after = land_a[s, 0], land_a[s, 1]
        m2_after, m1_after, _, _ = face_weights(land_w[1, s, 0], land_w[1, s, 1])
        _, _, m0_head, p1_head = face_weights(pack_w[1, s, 0], pack_w[1, s, 1])
        _, _, _, p1_before = face_weights(land_w[0, s, 0], land_w[0, s, 1])
        jump = after - jnp.where(even, roll(tail, lanes - 1), roll(after, 1))
        top = m2_after * jump + roll(jnp.where(even, m1_after * jump, 0.0), 1)
        top = jnp.where(my_lat < nlat - 1, top, 0.0)
        jump = jnp.where(even, head - roll(before, lanes - 1), before - roll(before, 1))
        flux = jnp.where(even, p1_head, p1_before) * jump
        low = jnp.where(even, m0_head * jump + roll(flux, lanes - 1), roll(flux, 1))
        low = roll(jnp.where(my_lat > 0, low, 0.0), 2)
        first = lax.rem(lane, 4) < 2
        both = (jnp.where(first, top, low), jnp.where(first, low, top))
        edge = jnp.logical_or(lane < 2, lane >= lanes - 2)

        def body(m, carry):
            for odd in range(2):
                level = 2 * m + odd
                turned = roll(both[odd], lanes - 2 - 2 * level)
                ext[s, level, OWN : OWN + rows] += jnp.where(edge, turned, 0.0)
            return carry

        lax.fori_loop(0, levels // 2, body, 0, unroll=True)

    def lon_own_weights(s):
        def body(level, carry):
            found = face_weights(
                lonc[s, level, OWN : OWN + rows], lonb[s, level, OWN : OWN + rows]
            )
            for member in range(4):
                lw[s, member, level, OWN : OWN + rows] = found[member]
            return carry

        lax.fori_loop(0, levels, body, 0, unroll=True)

    def lon_far_weights(s):
        def body(level, carry):
            found = face_weights(lonc[s, level, OWN - 2 : OWN], lonb[s, level, OWN - 2 : OWN])
            lw[s, 3, level, OWN - 2 : OWN] = found[3]
            end = OWN + rows
            found = face_weights(lonc[s, level, end : end + 2], lonb[s, level, end : end + 2])
            lw[s, 0, level, end : end + 2] = found[0]
            lw[s, 1, level, end : end + 2] = found[1]
            return carry

        lax.fori_loop(0, levels, body, 0, unroll=True)

    def lon_level(s, level):
        a = [ext[s, level, OWN + k : OWN + k + rows] for k in range(-2, 3)]
        w = [
            lw[s, member, level, OWN + 2 - member : OWN + 2 - member + rows]
            for member in range(4)
        ]
        out = a[2] + w[0] * (a[4] - a[3]) + w[1] * (a[3] - a[2])
        return out + w[2] * (a[2] - a[1]) + w[3] * (a[1] - a[0])

    def send_rows(buffer_at, at_dst, base):
        last = pl.ds(OWN + rows - 2, 2)
        return (
            remote(buffer_at(last), at_dst(pl.ds(OWN - 2, 2)), base, east),
            remote(buffer_at(pl.ds(OWN, 2)), at_dst(pl.ds(OWN + rows, 2)), base + 1, west),
        )

    def find_slots():
        order = order_ref[...]
        table = jnp.concatenate([order // 128, lax.rem(order, 128)], axis=0)
        table = table.astype(jnp.float32).astype(jnp.bfloat16)
        high = order.shape[0]
        down = lax.broadcasted_iota(jnp.int32, (lanes, lanes), 0)
        row_of = lax.broadcasted_iota(jnp.int32, (high, lanes), 0)
        for i in range(rows):
            region = rmap_ref[i : i + 1, :]
            hit = jnp.where(down == lax.rem(region, 128), 1.0, 0.0).astype(jnp.bfloat16)
            found = jnp.dot(table, hit, preferred_element_type=jnp.float32)
            here = row_of == region // 128
            hi = jnp.sum(jnp.where(here, found[:high], 0.0), axis=0, keepdims=True)
            lo = jnp.sum(jnp.where(here, found[high:], 0.0), axis=0, keepdims=True)
            hi_ref[i : i + 1, :] = hi
            cht[:, i * lanes : (i + 1) * lanes] = jnp.where(
                down.astype(jnp.float32) == lo, 1.0, 0.0
            ).astype(jnp.bfloat16)

    def regions(s, field):
        high = order_ref.shape[0]
        row_of = lax.broadcasted_iota(jnp.int32, (high, lanes), 0).astype(jnp.float32)
        lo_ref[...] = field
        for i in range(rows):
            here = row_of == hi_ref[i : i + 1, :]
            spread = jnp.where(here, lo_ref[i : i + 1, :], 0.0)
            coarse = spread.astype(jnp.bfloat16)
            fine = (spread - coarse.astype(jnp.float32)).astype(jnp.bfloat16)
            amat[:high, i * lanes : (i + 1) * lanes] = coarse
            amat[high:, i * lanes : (i + 1) * lanes] = fine
        sums = lax.dot_general(
            amat[...], cht[...], (((1,), (1,)), ((), ())), preferred_element_type=jnp.float32
        )
        pscr[...] = sums[:high] + sums[high:]
        for group in range(high // 2):
            send_ref[group, 2 * s : 2 * s + 2, :] = pscr[2 * group : 2 * group + 2, :]

    get_mix[1].wait()
    coefficients(1)
    get_latc.wait()
    get_latb.wait()
    for s in range(steps):
        pack_weights(s)
    get_adj.wait()
    solve(1)
    pl.semaphore_wait(barrier, count - 1)

    arriving = []
    lat_a = {}
    lat_a[1] = (
        remote(pack_a.at[1, 0], land_a.at[1, 0], 0, north),
        remote(pack_a.at[1, 1], land_a.at[1, 1], 1, south),
    )
    lat_w = (
        remote(pack_w.at[0], land_w.at[0], 2, north),
        remote(pack_w.at[1], land_w.at[1], 3, south),
    )
    get_lonc.wait()
    get_lonb.wait()
    lon_c = send_rows(
        lambda at: lonc.at[:, :, at, :], lambda at: lonc.at[:, :, at, :], 4
    )
    lon_b = send_rows(
        lambda at: lonb.at[:, :, at, :], lambda at: lonb.at[:, :, at, :], 6
    )
    lat_inner(1)
    lon_own_weights(1)
    for copy in lat_a[1] + lat_w:
        copy.wait_recv()
    lat_edges(1)
    lon_a = {}
    lon_a[1] = send_rows(
        lambda at: ext.at[1, :, at, :], lambda at: ext.at[1, :, at, :], 8
    )
    get_mix[0].wait()
    coefficients(0)
    find_slots()
    lon_own_weights(0)
    for copy in lon_c + lon_b:
        copy.wait_recv()
    for s in (1, 0):
        lon_far_weights(s)
    for copy in lon_a[1]:
        copy.wait_recv()

    def middle(level, carry):
        x_ref[level] = lon_level(1, level)
        return carry

    lax.fori_loop(0, levels, middle, 0, unroll=True)
    cosine = cos_ref[pl.ds(my_lat, 1), 0, :]
    solve(0)
    lat_a[0] = (
        remote(pack_a.at[0, 0], land_a.at[0, 0], 10, north),
        remote(pack_a.at[0, 1], land_a.at[0, 1], 11, south),
    )
    lat_inner(0)
    for copy in lat_a[0]:
        copy.wait_recv()
    lat_edges(0)
    lon_a[0] = send_rows(
        lambda at: ext.at[0, :, at, :], lambda at: ext.at[0, :, at, :], 12
    )
    regions(1, x_ref[0] * cosine)
    for copy in lon_a[0]:
        copy.wait_recv()
    start = lon_level(0, 0)
    out_ref[0] = start
    regions(0, start * cosine)

    def group_of(device):
        return (device * width) // blk

    def scatter(k, carry):
        device = lax.rem(me + k, count)
        pltpu.make_async_remote_copy(
            src_ref=send_ref.at[group_of(device)],
            dst_ref=land.at[me],
            send_sem=all_sem.at[0],
            recv_sem=all_sem.at[1],
            device_id=place(device),
            device_id_type=MESH,
        ).start()
        return carry

    lax.fori_loop(1, count, scatter, 0)
    land[me] = send_ref[group_of(me)]

    def last(level, carry):
        out_ref[level] = lon_level(0, level)
        return carry

    lax.fori_loop(1, levels, last, 0, unroll=True)
    get_cov.wait()
    for copy in lat_a[1] + lat_w + lon_c + lon_b + lon_a[1] + lat_a[0] + lon_a[0]:
        copy.wait_send()
    every = land.at[pl.ds(0, count - 1)]
    pltpu.make_async_copy(every, every, all_sem.at[0]).wait()
    pltpu.make_async_copy(every, every, all_sem.at[1]).wait()
    totals = jnp.sum(land[...], axis=0)
    half = blk // 2
    one = jnp.dot(
        totals, covv[:half], precision=lax.Precision.HIGHEST, preferred_element_type=jnp.float32
    )
    two = jnp.dot(
        totals, covv[half:], precision=lax.Precision.HIGHEST, preferred_element_type=jnp.float32
    )
    for s in range(steps):
        flux_ref[s : s + 1, :] = one[2 * s : 2 * s + 1] + two[2 * s + 1 : 2 * s + 2]


def per_device(
    nlon,
    nlat,
    adjoint_final,
    lon_courant,
    lon_branch,
    lat_courant,
    lat_branch,
    mixing,
    region_map,
    region_order,
    prior_cov,
):
    steps, levels, rows, lanes = lon_courant.shape
    regions = region_order.shape[0]
    blk = prior_cov.shape[1]
    width = regions // (nlon * nlat)
    lat_total = lanes * nlat
    lat_index = np.arange(lat_total, dtype=np.float32)
    angle = (lat_index + np.float32(0.5)) * np.float32(math.pi / lat_total)
    cosines = np.cos((angle - np.float32(0.5 * math.pi)).astype(np.float32))
    cosines = jnp.asarray(cosines.astype(np.float32).reshape(nlat, 1, lanes))
    f32, i32, b16 = jnp.float32, jnp.int32, jnp.bfloat16
    field = (levels, rows, lanes)
    tall = (levels, rows + 2 * OWN, lanes)
    vm = pltpu.VMEM
    scratch = [
        vm(field, f32),
        vm((steps, levels - 1, rows, lanes), f32),
        vm((steps,) + field, f32),
        vm((steps,) + field, i32),
        vm((steps,) + tall, f32),
        vm((steps,) + tall, i32),
        vm((blk, blk), f32),
        vm((steps,) + field, f32),
        vm((steps,) + field, f32),
        vm((steps,) + field, f32),
        vm(field, f32),
        vm((steps,) + tall, f32),
        vm((steps, 4) + tall, f32),
        vm((2, steps, 2, rows, lanes), f32),
        vm((2, steps, 2, rows, lanes), f32),
        vm((steps, 2, rows, lanes), f32),
        vm((steps, 2, rows, lanes), f32),
        vm((rows, lanes), f32),
        vm((rows, lanes), f32),
        vm((128, rows * lanes), b16),
        vm((2 * (regions // 128), rows * lanes), b16),
        vm((regions // 128, 128), f32),
        vm((regions // blk, 4, 128), f32),
        vm((nlon * nlat, 4, 128), f32),
        pltpu.SemaphoreType.DMA((8,)),
        pltpu.SemaphoreType.DMA((14,)),
        pltpu.SemaphoreType.DMA((14,)),
        pltpu.SemaphoreType.DMA((2,)),
    ]
    adjoint, flux = pl.pallas_call(
        functools.partial(kernel, nlon, nlat, width),
        out_shape=(
            jax.ShapeDtypeStruct(field, f32),
            jax.ShapeDtypeStruct((steps, blk), f32),
        ),
        in_specs=[pl.BlockSpec(memory_space=pl.ANY)] * 7
        + [pl.BlockSpec(memory_space=pltpu.VMEM)] * 3,
        out_specs=(
            pl.BlockSpec(memory_space=pltpu.VMEM),
            pl.BlockSpec(memory_space=pltpu.VMEM),
        ),
        scratch_shapes=scratch,
        compiler_params=pltpu.CompilerParams(
            collective_id=0, has_side_effects=True, vmem_limit_bytes=40 * 1024 * 1024
        ),
    )(
        adjoint_final,
        lon_courant,
        lon_branch,
        lat_courant,
        lat_branch,
        mixing,
        prior_cov,
        region_map,
        region_order.reshape(regions // 128, 128),
        cosines,
    )
    if width < blk:
        start = lax.rem(lax.axis_index("lat") * width, blk)
        flux = lax.dynamic_slice_in_dim(flux, start, width, 1)
    return adjoint, flux


def solution(mesh):
    four = P(None, None, "lon", "lat")
    placed = (
        P(None, "lon", "lat"),
        four,
        four,
        four,
        four,
        four,
        P("lon", "lat"),
        P(),
        P("lon", None, None),
    )
    return jax.shard_map(
        functools.partial(per_device, mesh.shape["lon"], mesh.shape["lat"]),
        mesh=mesh,
        in_specs=placed,
        out_specs=(P(None, "lon", "lat"), P(None, ("lon", "lat"))),
        check_vma=False,
    )
```

time: 260 us -> 37.5 us (0.14)
  waiting for transfers between devices: 148 us -> 0 us
  starting transfers between devices: 32.9 us -> 0 us
  Pallas kernels: 0 us -> 25.6 us
  local copies, waits for them, and re-layouts: 35.6 us -> 10.7 us
  other arithmetic: 21.8 us -> 0 us
  between operations: 15.1 us -> 0.66 us
  blocking collectives: 4.34 us -> 0 us
    unnamed x2 -> x0, waiting for transfers between devices: 140 us -> none
    ppermute x12 -> x0, starting transfers between devices: 32.9 us -> none  [the longest x6 17.1 us: extended(): lax.ppermute(tail, axis, [(i, (i + 1) % count) for i in range(ends)])]
    pallas_call x0 -> x1, Pallas kernels: none -> 25.6 us  [per_device(): pl.pallas_call(functools.partial(kernel, nlon, nlat, width), out_shape=(j...]
    gather x1 -> x0, local copies, waits for them, and re-layouts: 11.8 us -> none  [per_device(): slots = jnp.take(region_order, region_map.reshape(cell_count), axis=0)]
    ppermute x12 -> x0, waiting for transfers between devices: 8.32 us -> none  [the longest x6 5.93 us: extended(): lax.ppermute(tail, axis, [(i, (i + 1) % count) for i in range(ends)])]
    concatenate x6 -> x0, other arithmetic: 8.05 us -> none  [extended(): jnp.concatenate([lax.ppermute(tail, axis, [(i, (i + 1) % count) for i in...]
    slice x22 -> x0, local copies, waits for them, and re-layouts: 7.42 us -> none  [the longest x5 2.81 us: extended(): lax.slice_in_dim(cells, cells.shape[dim] - width, cells.shape[dim], axis=...]
    ppermute x2 -> x0, local copies, waits for them, and re-layouts: 6.63 us -> none  [the longest x1 3.32 us: extended(): lax.ppermute(head, axis, [((i + 1) % count, i) for i in range(ends)])]
  transfers between devices with their start and end apart: 13 -> 0, of which waited for: 5 -> 0; matrix products, arithmetic and copies ran while one was open for 16% -> 0% of each run, Pallas kernels for 0% -> 0%
where the time goes in v1:
time: 37.5 us; the launch traced here: 36.9 us
  Pallas kernels  25.6 us (68%)
  local copies, waits for them, and re-layouts  10.7 us (29%)
  between operations  0.66 us (2%)
    pallas_call x1, Pallas kernels, per_device(): pl.pallas_call(functools.partial(kernel, nlon, nlat, width), out_shape=(j...  25.6 us
    unnamed x22, local copies, waits for them, and re-layouts  10.7 us

profile of v1, /device:TPU:0, one launch (start us, length us, event | category | flops | bytes accessed | tf_op | source)
XLA Modules:
  0.0 36.9 jit_solution(6363386208431239130)
XLA Ops:
  0.6 0.0 copy-start.9
  0.6 0.7 %copy-done.9 = f32[2,1,128]{2,1,0:T(1,128)S(1)} copy-done((f32[2,1,128]{2,1,0:T(1,128)S(1)}, f32[2,1,128]{2,1,0:T(1,128)}, u32[]{:S(2)}) %copy-start.9) | copy-done | bytes 1048
  1.3 0.0 copy-start
  1.3 1.1 %copy-done = f32[2,34,16,128]{3,2,1,0:T(8,128)S(1)} copy-done((f32[2,34,16,128]{3,2,1,0:T(8,128)S(1)}, f32[2,34,16,128]{3,2,1,0:T(8,128)}, u32[]{:S(2)}) %copy-start) | copy-done | bytes 557080
  2.4 0.0 copy-start.1
  2.4 1.1 %copy-done.1 = s32[2,34,16,128]{3,2,1,0:T(8,128)S(1)} copy-done((s32[2,34,16,128]{3,2,1,0:T(8,128)S(1)}, s32[2,34,16,128]{3,2,1,0:T(8,128)}, u32[]{:S(2)}) %copy-start.1) | copy-done | bytes 557080
  3.4 0.0 copy-start.2
  3.4 1.1 %copy-done.2 = f32[2,34,16,128]{3,2,1,0:T(8,128)S(1)} copy-done((f32[2,34,16,128]{3,2,1,0:T(8,128)S(1)}, f32[2,34,16,128]{3,2,1,0:T(8,128)}, u32[]{:S(2)}) %copy-start.2) | copy-done | bytes 557080
  4.5 0.0 copy-start.3
  4.5 1.1 %copy-done.3 = s32[2,34,16,128]{3,2,1,0:T(8,128)S(1)} copy-done((s32[2,34,16,128]{3,2,1,0:T(8,128)S(1)}, s32[2,34,16,128]{3,2,1,0:T(8,128)}, u32[]{:S(2)}) %copy-start.3) | copy-done | bytes 557080
  5.5 0.0 copy-start.4
  5.5 1.0 %copy-done.4 = f32[2,33,16,128]{3,2,1,0:T(8,128)S(1)} copy-done((f32[2,33,16,128]{3,2,1,0:T(8,128)S(1)}, f32[2,33,16,128]{3,2,1,0:T(8,128)}, u32[]{:S(2)}) %copy-start.4) | copy-done | bytes 540696
  6.6 0.0 copy-start.5
  6.6 1.0 %copy-done.5 = f32[2,256,256]{2,1,0:T(8,128)S(1)} copy-done((f32[2,256,256]{2,1,0:T(8,128)S(1)}, f32[2,256,256]{2,1,0:T(8,128)}, u32[]{:S(2)}) %copy-start.5) | copy-done | bytes 524312
  7.6 0.0 copy-start.6
  7.6 1.0 %copy-done.6 = f32[34,16,128]{2,1,0:T(8,128)S(1)} copy-done((f32[34,16,128]{2,1,0:T(8,128)S(1)}, f32[34,16,128]{2,1,0:T(8,128)}, u32[]{:S(2)}) %copy-start.6) | copy-done | bytes 278552
  8.6 0.0 copy-start.7
  8.6 0.8 %copy-done.7 = s32[8192]{0:T(1024)S(1)} copy-done((s32[8192]{0:T(1024)S(1)}, s32[8192]{0:T(1024)}, u32[]{:S(2)}) %copy-start.7) | copy-done | bytes 32792
  9.3 0.0 copy-start.8
  9.3 0.7 %copy-done.8 = s32[16,128]{1,0:T(8,128)S(1)} copy-done((s32[16,128]{1,0:T(8,128)S(1)}, s32[16,128]{1,0:T(8,128)}, u32[]{:S(2)}) %copy-start.8) | copy-done | bytes 8216
  10.0 25.6 %shard_map.113 = (f32[34,16,128]{2,1,0:T(8,128)S(1)}, f32[2,256]{1,0:T(2,128)S(1)}) custom-call(f32[34,16,128]{2,1,0:T(8,128)S(1)} %copy-done.6, f32[2,34,16,128]{3,2,1,0:T(8,128)S(1)} %copy-done, s32[2,34,16,128]{3,2,1,0:T(8,128)S(1)} %copy-done.1, f32[2,34,16,128]{3,2,1,0:T(8,128)S(1)} %copy-done.2, s32[2,34,16,128]{3,2,1,0:T(8,128)S(1)} %copy-done.3, ...), custom_call_target="tpu_custom_call" | custom-call | tf_op jit(solution)/shard_map/pallas_call | solution.py:479
  35.6 0.7 %copy.14 = f32[34,16,128]{2,1,0:T(8,128)} copy(f32[34,16,128]{2,1,0:T(8,128)S(1)} %get-tuple-element.4) | data formatting | bytes 557056
  36.4 0.6 %copy.15 = f32[2,256]{1,0:T(2,128)} copy(f32[2,256]{1,0:T(2,128)S(1)} %get-tuple-element.5) | data formatting | bytes 4096
Async XLA Ops:
  0.6 0.7 %copy-start.9 = (f32[2,1,128]{2,1,0:T(1,128)S(1)}, f32[2,1,128]{2,1,0:T(1,128)}, u32[]{:S(2)}) copy-start(f32[2,1,128]{2,1,0:T(1,128)} %constant.2.clone.cos_ref) | copy-start | bytes 3076
  1.3 1.1 %copy-start = (f32[2,34,16,128]{3,2,1,0:T(8,128)S(1)}, f32[2,34,16,128]{3,2,1,0:T(8,128)}, u32[]{:S(2)}) copy-start(f32[2,34,16,128]{3,2,1,0:T(8,128)} %lonc_h.1) | copy-start | bytes 1671172
  2.4 1.1 %copy-start.1 = (s32[2,34,16,128]{3,2,1,0:T(8,128)S(1)}, s32[2,34,16,128]{3,2,1,0:T(8,128)}, u32[]{:S(2)}) copy-start(s32[2,34,16,128]{3,2,1,0:T(8,128)} %lonb_h.1) | copy-start | bytes 1671172
  3.4 1.1 %copy-start.2 = (f32[2,34,16,128]{3,2,1,0:T(8,128)S(1)}, f32[2,34,16,128]{3,2,1,0:T(8,128)}, u32[]{:S(2)}) copy-start(f32[2,34,16,128]{3,2,1,0:T(8,128)} %latc_h.1) | copy-start | bytes 1671172
  4.5 1.1 %copy-start.3 = (s32[2,34,16,128]{3,2,1,0:T(8,128)S(1)}, s32[2,34,16,128]{3,2,1,0:T(8,128)}, u32[]{:S(2)}) copy-start(s32[2,34,16,128]{3,2,1,0:T(8,128)} %latb_h.1) | copy-start | bytes 1671172
  5.5 1.0 %copy-start.4 = (f32[2,33,16,128]{3,2,1,0:T(8,128)S(1)}, f32[2,33,16,128]{3,2,1,0:T(8,128)}, u32[]{:S(2)}) copy-start(f32[2,33,16,128]{3,2,1,0:T(8,128)} %mix_h.1) | copy-start | bytes 1622020
  6.6 1.0 %copy-start.5 = (f32[2,256,256]{2,1,0:T(8,128)S(1)}, f32[2,256,256]{2,1,0:T(8,128)}, u32[]{:S(2)}) copy-start(f32[2,256,256]{2,1,0:T(8,128)} %cov_h.1) | copy-start | bytes 1572868
  7.6 1.0 %copy-start.6 = (f32[34,16,128]{2,1,0:T(8,128)S(1)}, f32[34,16,128]{2,1,0:T(8,128)}, u32[]{:S(2)}) copy-start(f32[34,16,128]{2,1,0:T(8,128)} %adj_h.1) | copy-start | bytes 835588
  8.6 0.8 %copy-start.7 = (s32[8192]{0:T(1024)S(1)}, s32[8192]{0:T(1024)}, u32[]{:S(2)}) copy-start(s32[8192]{0:T(1024)} %param.17) | copy-start | bytes 98308
  9.3 0.7 %copy-start.8 = (s32[16,128]{1,0:T(8,128)S(1)}, s32[16,128]{1,0:T(8,128)}, u32[]{:S(2)}) copy-start(s32[16,128]{1,0:T(8,128)} %rmap_ref.1) | copy-start | bytes 24580

commit v2 on v1

--- a/solution.py
+++ b/solution.py
@@ -38,11 +38,14 @@
     latb_h,
     mix_h,
     cov_h,
+    rmap_h,
+    order_h,
+    cos_h,
+    out_ref,
+    flux_ref,
     rmap_ref,
     order_ref,
     cos_ref,
-    out_ref,
-    flux_ref,
     x_ref,
     mixv,
     latc,
@@ -60,6 +63,11 @@
     land_w,
     pack_a,
     land_a,
+    rows_a,
+    far_a,
+    rows_w,
+    far_w,
+    far_out,
     hi_ref,
     lo_ref,
     cht,
@@ -106,6 +114,11 @@
     get_lonb = fetch(lonb_h, lonb.at[:, :, own, :], 5)
     get_mix[0] = fetch(mix_h.at[0], mixv.at[0], 6)
     get_cov = fetch(cov_h.at[(my_lat * width) // blk], covv, 7)
+    get_small = (
+        fetch(rmap_h, rmap_ref, 8),
+        fetch(order_h, order_ref, 9),
+        fetch(cos_h.at[my_lat], cos_ref, 10),
+    )
 
     lane = lax.broadcasted_iota(jnp.int32, (rows, lanes), 1)
     pair = lane // 2
@@ -172,39 +185,64 @@
             level = levels - 1 - i
             value = y_ref[level] + nr_ref[s, level] * value
             y_ref[level] = value
+            rows_a[0, s, pl.ds(2 * level, 2), :] = value[rows - 2 :]
+            rows_a[1, s, pl.ds(2 * level, 2), :] = value[:2]
             return (value,) + tail_head(value, level, tail, head)
 
         _, tail, head = lax.fori_loop(0, levels, down, (zero, zero, zero), unroll=True)
-        pack_a[s, 0] = tail
-        pack_a[s, 1] = roll(head, lanes - 2)
+        head = roll(head, lanes - 2)
+        for member, value in enumerate((tail, head)):
+            pack_a[s, member, OWN : OWN + rows] = value
+            at = 2 * levels + 2 * member
+            rows_a[0, s, at : at + 2] = value[rows - 2 :]
+            rows_a[1, s, at : at + 2] = value[:2]
 
     def pack_weights(s):
         def body(level, carry):
             ct, ch, bt, bh = carry
             ct, ch = tail_head(latc[s, level], level, ct, ch)
-            bt, bh = tail_head(latb[s, level].astype(jnp.float32), level, bt, bh)
+            both = (latc[s, level], latb[s, level].astype(jnp.float32))
+            bt, bh = tail_head(both[1], level, bt, bh)
+            for member in range(2):
+                rows_w[0, s, member, pl.ds(2 * level, 2), :] = both[member][rows - 2 :]
+                rows_w[1, s, member, pl.ds(2 * level, 2), :] = both[member][:2]
             return ct, ch, bt, bh
 
         ct, ch, bt, bh = lax.fori_loop(0, levels, body, (zero,) * 4, unroll=True)
-        pack_w[0, s, 0] = ct
-        pack_w[0, s, 1] = bt
-        pack_w[1, s, 0] = roll(ch, lanes - 2)
-        pack_w[1, s, 1] = roll(bh, lanes - 2)
+        found = ((ct, bt), (roll(ch, lanes - 2), roll(bh, lanes - 2)))
+        for end in range(2):
+            at = 2 * levels + 2 * end
+            for member in range(2):
+                value = found[end][member]
+                pack_w[end, s, member, OWN : OWN + rows] = value
+                rows_w[0, s, member, at : at + 2] = value[rows - 2 :]
+                rows_w[1, s, member, at : at + 2] = value[:2]
+
+    def lat_pass(a, courant, branch):
+        at = lax.broadcasted_iota(jnp.int32, a.shape, 1)
+        m2, m1, m0, p1 = face_weights(courant, branch)
+        jump = jnp.where(at >= 1, a - roll(a, 1), 0.0)
+        out = a + m0 * jump + roll(m1 * jump, lanes - 1)
+        out = out + roll(jnp.where(at >= 2, m2 * jump, 0.0), lanes - 2)
+        return out + roll(jnp.where(at <= lanes - 2, p1 * jump, 0.0), 1)
 
     def lat_inner(s):
         def body(level, carry):
-            a = y_ref[level]
-            m2, m1, m0, p1 = face_weights(latc[s, level], latb[s, level])
-            jump = jnp.where(lane >= 1, a - roll(a, 1), 0.0)
-            out = a + m0 * jump + roll(m1 * jump, lanes - 1)
-            out = out + roll(jnp.where(lane >= 2, m2 * jump, 0.0), lanes - 2)
-            out = out + roll(jnp.where(lane <= lanes - 2, p1 * jump, 0.0), 1)
+            out = lat_pass(y_ref[level], latc[s, level], latb[s, level])
             ext[s, level, OWN : OWN + rows] = out
             return carry
 
         lax.fori_loop(0, levels, body, 0, unroll=True)
 
     def lat_edges(s):
+        at = 2 * levels
+        lane = lax.broadcasted_iota(jnp.int32, (rows + 2 * OWN, lanes), 1)
+        even = lax.rem(lane, 2) == 0
+        for side, where in enumerate((slice(OWN - 2, OWN), slice(OWN + rows, OWN + rows + 2))):
+            far_out[side] = lat_pass(far_a[side, s], far_w[side, s, 0], far_w[side, s, 1])
+            for member in range(2):
+                pack_a[s, member, where] = far_a[side, s, at + 2 * member : at + 2 * member + 2]
+                pack_w[1, s, member, where] = far_w[side, s, member, at + 2 : at + 4]
         tail, head = pack_a[s, 0], pack_a[s, 1]
         before, after = land_a[s, 0], land_a[s, 1]
         m2_after, m1_after, _, _ = face_weights(land_w[1, s, 0], land_w[1, s, 1])
@@ -224,8 +262,12 @@
         def body(m, carry):
             for odd in range(2):
                 level = 2 * m + odd
-                turned = roll(both[odd], lanes - 2 - 2 * level)
-                ext[s, level, OWN : OWN + rows] += jnp.where(edge, turned, 0.0)
+                turned = jnp.where(edge, roll(both[odd], lanes - 2 - 2 * level), 0.0)
+                ext[s, level, OWN : OWN + rows] += turned[OWN : OWN + rows]
+                two = pl.ds(2 * level, 2)
+                end = OWN + rows
+                ext[s, level, OWN - 2 : OWN] = far_out[0, two, :] + turned[OWN - 2 : OWN]
+                ext[s, level, end : end + 2] = far_out[1, two, :] + turned[end : end + 2]
             return carry
 
         lax.fori_loop(0, levels // 2, body, 0, unroll=True)
@@ -316,65 +358,83 @@
     solve(1)
     pl.semaphore_wait(barrier, count - 1)
 
-    arriving = []
-    lat_a = {}
-    lat_a[1] = (
-        remote(pack_a.at[1, 0], land_a.at[1, 0], 0, north),
-        remote(pack_a.at[1, 1], land_a.at[1, 1], 1, south),
-    )
-    lat_w = (
-        remote(pack_w.at[0], land_w.at[0], 2, north),
-        remote(pack_w.at[1], land_w.at[1], 3, south),
+    turn = {1: lax.rem(my_lon + 1, nlon), -1: lax.rem(my_lon + nlon - 1, nlon)}
+    own_rows, first, last_two = pl.ds(OWN, rows), pl.ds(OWN, 2), pl.ds(OWN + rows - 2, 2)
+    low, high = pl.ds(OWN - 2, 2), pl.ds(OWN + rows, 2)
+
+    def send_columns(source, target, base):
+        copies = []
+        for end in range(2):
+            beside = (north, south)[end][1]
+            for k, (lon, src, dst) in enumerate(
+                (
+                    (my_lon, own_rows, own_rows),
+                    (turn[1], last_two, low),
+                    (turn[-1], first, high),
+                )
+            ):
+                copies.append(
+                    remote(source(end, src), target(end, dst), base + 3 * end + k, (lon, beside))
+                )
+        return tuple(copies)
+
+    def exchange(s, base):
+        return (
+            remote(rows_a.at[0, s], far_a.at[0, s], base, east),
+            remote(rows_a.at[1, s], far_a.at[1, s], base + 1, west),
+        ) + send_columns(
+            lambda end, at: pack_a.at[s, end, at, :],
+            lambda end, at: land_a.at[s, end, at, :],
+            base + 2,
+        )
+
+    def send_far_weights(s, base):
+        return (
+            remote(rows_w.at[0, s], far_w.at[0, s], base, east),
+            remote(rows_w.at[1, s], far_w.at[1, s], base + 1, west),
+        )
+
+    sent_a = {1: exchange(1, 0)}
+    sent_w = {1: send_far_weights(1, 8)}
+    lat_w = send_columns(
+        lambda end, at: pack_w.at[end, :, :, at, :],
+        lambda end, at: land_w.at[end, :, :, at, :],
+        10,
     )
     get_lonc.wait()
     get_lonb.wait()
-    lon_c = send_rows(
-        lambda at: lonc.at[:, :, at, :], lambda at: lonc.at[:, :, at, :], 4
-    )
-    lon_b = send_rows(
-        lambda at: lonb.at[:, :, at, :], lambda at: lonb.at[:, :, at, :], 6
-    )
+    lon_c = send_rows(lambda at: lonc.at[:, :, at, :], lambda at: lonc.at[:, :, at, :], 16)
+    lon_b = send_rows(lambda at: lonb.at[:, :, at, :], lambda at: lonb.at[:, :, at, :], 18)
+    sent_w[0] = send_far_weights(0, 20)
     lat_inner(1)
     lon_own_weights(1)
-    for copy in lat_a[1] + lat_w:
+    get_mix[0].wait()
+    coefficients(0)
+    for copy in sent_a[1] + sent_w[1] + lat_w:
         copy.wait_recv()
     lat_edges(1)
-    lon_a = {}
-    lon_a[1] = send_rows(
-        lambda at: ext.at[1, :, at, :], lambda at: ext.at[1, :, at, :], 8
-    )
-    get_mix[0].wait()
-    coefficients(0)
-    find_slots()
-    lon_own_weights(0)
     for copy in lon_c + lon_b:
         copy.wait_recv()
-    for s in (1, 0):
-        lon_far_weights(s)
-    for copy in lon_a[1]:
-        copy.wait_recv()
+    lon_far_weights(1)
 
     def middle(level, carry):
         x_ref[level] = lon_level(1, level)
         return carry
 
     lax.fori_loop(0, levels, middle, 0, unroll=True)
-    cosine = cos_ref[pl.ds(my_lat, 1), 0, :]
     solve(0)
-    lat_a[0] = (
-        remote(pack_a.at[0, 0], land_a.at[0, 0], 10, north),
-        remote(pack_a.at[0, 1], land_a.at[0, 1], 11, south),
-    )
+    sent_a[0] = exchange(0, 22)
     lat_inner(0)
-    for copy in lat_a[0]:
+    lon_own_weights(0)
+    lon_far_weights(0)
+    for copy in get_small:
+        copy.wait()
+    cosine = cos_ref[...]
+    find_slots()
+    regions(1, x_ref[0] * cosine)
+    for copy in sent_a[0] + sent_w[0]:
         copy.wait_recv()
     lat_edges(0)
-    lon_a[0] = send_rows(
-        lambda at: ext.at[0, :, at, :], lambda at: ext.at[0, :, at, :], 12
-    )
-    regions(1, x_ref[0] * cosine)
-    for copy in lon_a[0]:
-        copy.wait_recv()
     start = lon_level(0, 0)
     out_ref[0] = start
     regions(0, start * cosine)
@@ -403,7 +463,7 @@
 
     lax.fori_loop(1, levels, last, 0, unroll=True)
     get_cov.wait()
-    for copy in lat_a[1] + lat_w + lon_c + lon_b + lon_a[1] + lat_a[0] + lon_a[0]:
+    for copy in sent_a[1] + sent_a[0] + sent_w[1] + sent_w[0] + lat_w + lon_c + lon_b:
         copy.wait_send()
     every = land.at[pl.ds(0, count - 1)]
     pltpu.make_async_copy(every, every, all_sem.at[0]).wait()
@@ -447,6 +507,9 @@
     tall = (levels, rows + 2 * OWN, lanes)
     vm = pltpu.VMEM
     scratch = [
+        vm((rows, lanes), i32),
+        vm((regions // 128, 128), i32),
+        vm((1, lanes), f32),
         vm(field, f32),
         vm((steps, levels - 1, rows, lanes), f32),
         vm((steps,) + field, f32),
@@ -460,10 +523,15 @@
         vm(field, f32),
         vm((steps,) + tall, f32),
         vm((steps, 4) + tall, f32),
-        vm((2, steps, 2, rows, lanes), f32),
-        vm((2, steps, 2, rows, lanes), f32),
-        vm((steps, 2, rows, lanes), f32),
-        vm((steps, 2, rows, lanes), f32),
+        vm((2, steps, 2, rows + 2 * OWN, lanes), f32),
+        vm((2, steps, 2, rows + 2 * OWN, lanes), f32),
+        vm((steps, 2, rows + 2 * OWN, lanes), f32),
+        vm((steps, 2, rows + 2 * OWN, lanes), f32),
+        vm((2, steps, 2 * levels + 4, lanes), f32),
+        vm((2, steps, 2 * levels + 4, lanes), f32),
+        vm((2, steps, 2, 2 * levels + 4, lanes), f32),
+        vm((2, steps, 2, 2 * levels + 4, lanes), f32),
+        vm((2, 2 * levels + 4, lanes), f32),
         vm((rows, lanes), f32),
         vm((rows, lanes), f32),
         vm((128, rows * lanes), b16),
@@ -471,9 +539,9 @@
         vm((regions // 128, 128), f32),
         vm((regions // blk, 4, 128), f32),
         vm((nlon * nlat, 4, 128), f32),
-        pltpu.SemaphoreType.DMA((8,)),
-        pltpu.SemaphoreType.DMA((14,)),
-        pltpu.SemaphoreType.DMA((14,)),
+        pltpu.SemaphoreType.DMA((11,)),
+        pltpu.SemaphoreType.DMA((30,)),
+        pltpu.SemaphoreType.DMA((30,)),
         pltpu.SemaphoreType.DMA((2,)),
     ]
     adjoint, flux = pl.pallas_call(
@@ -482,15 +550,14 @@
             jax.ShapeDtypeStruct(field, f32),
             jax.ShapeDtypeStruct((steps, blk), f32),
         ),
-        in_specs=[pl.BlockSpec(memory_space=pl.ANY)] * 7
-        + [pl.BlockSpec(memory_space=pltpu.VMEM)] * 3,
+        in_specs=[pl.BlockSpec(memory_space=pltpu.HBM)] * 10,
         out_specs=(
             pl.BlockSpec(memory_space=pltpu.VMEM),
             pl.BlockSpec(memory_space=pltpu.VMEM),
         ),
         scratch_shapes=scratch,
         compiler_params=pltpu.CompilerParams(
-            collective_id=0, has_side_effects=True, vmem_limit_bytes=40 * 1024 * 1024
+            collective_id=0, has_side_effects=True, vmem_limit_bytes=61 * 1024 * 1024
         ),
     )(
         adjoint_final,

time: 37.5 us -> 28.6 us (0.76); the launches traced: 36.9 us -> 28.4 us
  local copies, waits for them, and re-layouts: 10.7 us -> 2.26 us
    unnamed x22 -> x4, local copies, waits for them, and re-layouts: 10.7 us -> 2.26 us
where the time goes in v2:
time: 28.6 us; the launch traced here: 28.4 us
  Pallas kernels  25.5 us (89%)
  local copies, waits for them, and re-layouts  2.26 us (8%)
  between operations  0.65 us (2%)
    pallas_call x1, Pallas kernels, per_device(): pl.pallas_call(functools.partial(kernel, nlon, nlat, width), out_shape=(j...  25.5 us
    unnamed x4, local copies, waits for them, and re-layouts  2.26 us

profile of v2, /device:TPU:0, one launch (start us, length us, event | category | flops | bytes accessed | tf_op | source)
XLA Modules:
  0.0 28.4 jit_solution(17874486077694216744)
XLA Ops:
  0.6 25.5 %shard_map.113 = (f32[34,16,128]{2,1,0:T(8,128)}, f32[2,256]{1,0:T(2,128)}) custom-call(f32[34,16,128]{2,1,0:T(8,128)} %adj_h.1, f32[2,34,16,128]{3,2,1,0:T(8,128)} %lonc_h.1, s32[2,34,16,128]{3,2,1,0:T(8,128)} %lonb_h.1, f32[2,34,16,128]{3,2,1,0:T(8,128)} %latc_h.1, s32[2,34,16,128]{3,2,1,0:T(8,128)} %latb_h.1, f32[2,33,16,128]{3,2,1,0:T(8,128)} %mix_h.1, ...), custom_call_target="tpu_custom_call" | custom-call | tf_op jit(solution)/shard_map/pallas_call | solution.py:547
  26.1 0.0 copy-start
  26.1 1.7 %copy.14 = f32[34,16,128]{2,1,0:T(8,128)} copy(f32[34,16,128]{2,1,0:T(8,128)} %get-tuple-element.4) | data formatting | bytes 557056
  27.8 0.0 copy-done
  27.8 0.6 %copy.15 = f32[2,256]{1,0:T(2,128)} copy(f32[2,256]{1,0:T(2,128)S(1)} %copy-done) | data formatting | bytes 4096
Async XLA Ops:
  26.1 1.7 %copy-start = (f32[2,256]{1,0:T(2,128)S(1)}, f32[2,256]{1,0:T(2,128)}, u32[]{:S(2)}) copy-start(f32[2,256]{1,0:T(2,128)} %get-tuple-element.5) | copy-start | bytes 6148

commit v3 on v2

--- a/solution.py
+++ b/solution.py
@@ -403,17 +403,23 @@
     )
     get_lonc.wait()
     get_lonb.wait()
-    lon_c = send_rows(lambda at: lonc.at[:, :, at, :], lambda at: lonc.at[:, :, at, :], 16)
-    lon_b = send_rows(lambda at: lonb.at[:, :, at, :], lambda at: lonb.at[:, :, at, :], 18)
-    sent_w[0] = send_far_weights(0, 20)
+
+    def send_lon(s, base):
+        return send_rows(
+            lambda at: lonc.at[s, :, at, :], lambda at: lonc.at[s, :, at, :], base
+        ) + send_rows(lambda at: lonb.at[s, :, at, :], lambda at: lonb.at[s, :, at, :], base + 2)
+
+    sent_lon = {1: send_lon(1, 16)}
     lat_inner(1)
     lon_own_weights(1)
     get_mix[0].wait()
     coefficients(0)
     for copy in sent_a[1] + sent_w[1] + lat_w:
         copy.wait_recv()
+    sent_w[0] = send_far_weights(0, 20)
+    sent_lon[0] = send_lon(0, 30)
     lat_edges(1)
-    for copy in lon_c + lon_b:
+    for copy in sent_lon[1]:
         copy.wait_recv()
     lon_far_weights(1)
 
@@ -426,12 +432,14 @@
     sent_a[0] = exchange(0, 22)
     lat_inner(0)
     lon_own_weights(0)
-    lon_far_weights(0)
     for copy in get_small:
         copy.wait()
     cosine = cos_ref[...]
     find_slots()
     regions(1, x_ref[0] * cosine)
+    for copy in sent_lon[0]:
+        copy.wait_recv()
+    lon_far_weights(0)
     for copy in sent_a[0] + sent_w[0]:
         copy.wait_recv()
     lat_edges(0)
@@ -463,7 +471,7 @@
 
     lax.fori_loop(1, levels, last, 0, unroll=True)
     get_cov.wait()
-    for copy in sent_a[1] + sent_a[0] + sent_w[1] + sent_w[0] + lat_w + lon_c + lon_b:
+    for copy in sent_a[1] + sent_a[0] + sent_w[1] + sent_w[0] + lat_w + sent_lon[1] + sent_lon[0]:
         copy.wait_send()
     every = land.at[pl.ds(0, count - 1)]
     pltpu.make_async_copy(every, every, all_sem.at[0]).wait()
@@ -540,15 +548,15 @@
         vm((regions // blk, 4, 128), f32),
         vm((nlon * nlat, 4, 128), f32),
         pltpu.SemaphoreType.DMA((11,)),
-        pltpu.SemaphoreType.DMA((30,)),
-        pltpu.SemaphoreType.DMA((30,)),
+        pltpu.SemaphoreType.DMA((34,)),
+        pltpu.SemaphoreType.DMA((34,)),
         pltpu.SemaphoreType.DMA((2,)),
     ]
     adjoint, flux = pl.pallas_call(
         functools.partial(kernel, nlon, nlat, width),
         out_shape=(
-            jax.ShapeDtypeStruct(field, f32),
-            jax.ShapeDtypeStruct((steps, blk), f32),
+            pltpu.VMEM(field, f32),
+            pltpu.VMEM((steps, blk), f32),
         ),
         in_specs=[pl.BlockSpec(memory_space=pltpu.HBM)] * 10,
         out_specs=(

time: 28.6 us -> 26.9 us (0.941)
  local copies, waits for them, and re-layouts: 2.26 us -> 1.29 us
  Pallas kernels: 25.5 us -> 24.9 us
    unnamed x4 -> x2, local copies, waits for them, and re-layouts: 2.26 us -> 1.29 us
    pallas_call x1, Pallas kernels: 25.5 us -> 24.9 us  [per_device(): pl.pallas_call(functools.partial(kernel, nlon, nlat, width), out_shape=(p...]
where the time goes in v3:
time: 26.9 us; the launch traced here: 26.8 us
  Pallas kernels  24.9 us (93%)
  local copies, waits for them, and re-layouts  1.29 us (5%)
  between operations  0.64 us (2%)
    pallas_call x1, Pallas kernels, per_device(): pl.pallas_call(functools.partial(kernel, nlon, nlat, width), out_shape=(p...  24.9 us
    unnamed x2, local copies, waits for them, and re-layouts  1.29 us

profile of v3, /device:TPU:0, one launch (start us, length us, event | category | flops | bytes accessed | tf_op | source)
XLA Modules:
  0.0 26.8 jit_solution(8813653943924274889)
XLA Ops:
  0.6 24.9 %shard_map.113 = (f32[34,16,128]{2,1,0:T(8,128)S(1)}, f32[2,256]{1,0:T(2,128)S(1)}) custom-call(f32[34,16,128]{2,1,0:T(8,128)} %adj_h.1, f32[2,34,16,128]{3,2,1,0:T(8,128)} %lonc_h.1, s32[2,34,16,128]{3,2,1,0:T(8,128)} %lonb_h.1, f32[2,34,16,128]{3,2,1,0:T(8,128)} %latc_h.1, s32[2,34,16,128]{3,2,1,0:T(8,128)} %latb_h.1, f32[2,33,16,128]{3,2,1,0:T(8,128)} %mix_h.1, ...), custom_call_target="tpu_custom_call" | custom-call | tf_op jit(solution)/shard_map/pallas_call | solution.py:555
  25.5 0.7 %copy.14 = f32[34,16,128]{2,1,0:T(8,128)} copy(f32[34,16,128]{2,1,0:T(8,128)S(1)} %get-tuple-element.2) | data formatting | bytes 557056
  26.2 0.6 %copy.15 = f32[2,256]{1,0:T(2,128)} copy(f32[2,256]{1,0:T(2,128)S(1)} %get-tuple-element.3) | data formatting | bytes 4096
